TPU v7x, 32 devices: a whole 2x2x4 slice. The times are simulated.
32 devices in a mesh: batch: 4 (over x, core), seq: 8 (over z, y).
Axes of the slice: x: 2, y: 2, z: 4, core: 2. Of those that a mesh axis runs over, the one named last changes fastest.
Arguments:
- tokens: bfloat16 [4, 2560, 512], P('batch', 'seq'), may hold values from -6 to 6
- norm_gains: float32 [2, 2, 512], replicated, may hold values from 0.25 to 1.75
- qkv_weight: bfloat16 [2, 512, 1536], replicated, may hold values from -0.25 to 0.25
- out_weight: bfloat16 [2, 512, 512], replicated, may hold values from -3.5 to 3.5
- up_weight: bfloat16 [2, 512, 2048], replicated, may hold values from -0.25 to 0.25
- down_weight: bfloat16 [2, 2048, 512], replicated, may hold values from -0.125 to 0.125
- gen_cotangent: bfloat16 [4, 2560, 512], P('batch', 'seq'), may hold values from -6 to 6
- disc_cotangent: bfloat16 [4, 2560, 512], P('batch', 'seq'), may hold values from -6 to 6
- seg_lengths: int32 [4, 4], P('batch'), may hold values from 0 to 2558, as said below
Outputs:
- gen_out: bfloat16 [4, 2560, 512], P('batch', 'seq')
- disc_out: bfloat16 [4, 2560, 512], P('batch', 'seq')
- gen_in_grad: bfloat16 [4, 2560, 512], P('batch', 'seq')
- disc_in_grad: bfloat16 [4, 2560, 512], P('batch', 'seq')
- gain_grad: float32 [2, 2, 512], replicated
- qkv_grad: float32 [2, 512, 1536], replicated
- out_grad: float32 [2, 512, 512], replicated
- up_grad: float32 [2, 512, 2048], replicated
- down_grad: float32 [2, 2048, 512], replicated
Inputs may be any that keep to these rules, and one draw needn't show every extreme that they name: `seg_lengths`: each row holds, for one pack, the lengths of a leading thumbnail (1 to min(256, 160) tokens), of one image, of a trailing thumbnail (1 to half of that) and of the padding (0 to a quarter of it), in this order; they sum to 2560. The image starts in the first band of seq and ends in the last. In one pack of each draw both thumbnails have one token and there is no padding.
All inputs are finite; a program needn't handle non-finite values.
Results may differ from a plain program's by a relative error of at most 0.015.
Values may be sent and summed in bfloat16 or wider, within the bound.
A program may use at most 320 MiB of HBM per device.

v0:
```python
import math

import jax
import jax.numpy as jnp
from jax import lax
from jax.sharding import PartitionSpec as P

HEADS = 8


epsilon = 1e-05
masked_score = -1e30
key_block = 2048


def layer_norm(inputs, gain_row):
    average = jnp.mean(inputs, axis=-1, keepdims=True)
    centred = inputs - average
    variance = jnp.mean(centred * centred, axis=-1, keepdims=True)
    return centred * lax.rsqrt(variance + epsilon) * gain_row


def gelu_tanh(inputs):
    return (
        0.5
        * inputs
        * (1.0 + jnp.tanh(0.7978845608028654 * (inputs + 0.044715 * inputs * inputs * inputs)))
    )


def segment_of(lengths, positions):
    first = lengths[0]
    second = first + lengths[1]
    third = second + lengths[2]
    return (
        (positions >= first).astype(jnp.int32)
        + (positions >= second).astype(jnp.int32)
        + (positions >= third).astype(jnp.int32)
    )


def block_scores(query_heads, key_heads, query_segment, key_segment, scale):
    scores = (
        jnp.einsum("qhe,khe->hqk", query_heads, key_heads, preferred_element_type=jnp.float32)
        * scale
    )
    allowed = query_segment[:, None] == key_segment[None, :]
    return jnp.where(allowed[None], scores, masked_score)


def split_blocks(array_rows, width):
    return array_rows.reshape((array_rows.shape[0] // width, width) + array_rows.shape[1:])


def attend(query_heads, key_heads, value_heads, query_segment, key_segment, scale):
    width = math.gcd(key_heads.shape[0], key_block)
    blocks = (
        split_blocks(key_heads, width),
        split_blocks(value_heads, width),
        split_blocks(key_segment, width),
    )
    heads = query_heads.shape[1]
    row_count = query_heads.shape[0]

    def statistics(carry, item):
        row_max, totals = carry
        scores = block_scores(query_heads, item[0], query_segment, item[2], scale)
        new_max = jnp.maximum(row_max, jnp.max(scores, axis=-1))
        totals = totals * jnp.exp(row_max - new_max) + jnp.sum(
            jnp.exp(scores - new_max[..., None]), axis=-1
        )
        return ((new_max, totals), None)

    start_max = jnp.full((heads, row_count), masked_score, jnp.float32)
    (row_max, totals), unused = lax.scan(
        statistics, (start_max, jnp.zeros((heads, row_count), jnp.float32)), blocks
    )
    log_total = row_max + jnp.log(totals)

    def weighted(running, item):
        scores = block_scores(query_heads, item[0], query_segment, item[2], scale)
        weights_low = jnp.exp(scores - log_total[..., None]).astype(jnp.bfloat16)
        return (
            running
            + jnp.einsum("hqk,khe->qhe", weights_low, item[1], preferred_element_type=jnp.float32),
            None,
        )

    attended, unused = lax.scan(weighted, jnp.zeros(query_heads.shape, jnp.float32), blocks)
    return (attended, log_total)


def query_side(
    query_heads,
    key_heads,
    value_heads,
    query_segment,
    key_segment,
    grad_heads,
    log_total,
    delta,
    scale,
):
    width = math.gcd(key_heads.shape[0], key_block)
    blocks = (
        split_blocks(key_heads, width),
        split_blocks(value_heads, width),
        split_blocks(key_segment, width),
    )

    def step(running, item):
        scores = block_scores(query_heads, item[0], query_segment, item[2], scale)
        weights = jnp.exp(scores - log_total[..., None])
        dprobs = jnp.einsum("qhe,khe->hqk", grad_heads, item[1], preferred_element_type=jnp.float32)
        dscores = (weights * (dprobs - delta[..., None])).astype(jnp.bfloat16)
        running = running + jnp.einsum(
            "hqk,khe->qhe", dscores, item[0], preferred_element_type=jnp.float32
        )
        key_part = (
            jnp.einsum("hqk,qhe->khe", dscores, query_heads, preferred_element_type=jnp.float32)
            * scale
        )
        value_part = jnp.einsum(
            "hqk,qhe->khe",
            weights.astype(jnp.bfloat16),
            grad_heads,
            preferred_element_type=jnp.float32,
        )
        return (running, (key_part, value_part))

    grad_query, key_parts = lax.scan(step, jnp.zeros(query_heads.shape, jnp.float32), blocks)
    return (grad_query * scale, key_parts)


def block_forward(inputs, gains, qkv_matrix, out_matrix, up_matrix, down_matrix, lengths):
    row_count, width = inputs.shape
    heads = HEADS
    head_size = width // heads
    scale = head_size ** (-0.5)
    band_index = lax.axis_index("seq")
    positions = band_index * row_count + jnp.arange(row_count, dtype=jnp.int32)
    query_segment = segment_of(lengths, positions)
    key_segment = segment_of(lengths, jnp.arange(row_count * lax.axis_size("seq"), dtype=jnp.int32))
    keep_rows = (query_segment < 3).astype(jnp.float32)[:, None]
    normed = layer_norm(inputs, gains[0]).astype(jnp.bfloat16)
    qkv_rows = jnp.dot(normed, qkv_matrix, preferred_element_type=jnp.float32).astype(jnp.bfloat16)
    all_keys, all_values = (
        lax.all_gather(qkv_rows[:, width : 2 * width], "seq", axis=0, tiled=True),
        lax.all_gather(qkv_rows[:, 2 * width :], "seq", axis=0, tiled=True),
    )
    attended, log_total = attend(
        qkv_rows[:, :width].reshape(row_count, heads, head_size),
        all_keys.reshape(-1, heads, head_size),
        all_values.reshape(-1, heads, head_size),
        query_segment,
        key_segment,
        scale,
    )
    attended = attended.reshape(row_count, width)
    attended_low = (attended * keep_rows).astype(jnp.bfloat16)
    middle = inputs + jnp.dot(attended_low, out_matrix, preferred_element_type=jnp.float32)
    second_norm = layer_norm(middle, gains[1]).astype(jnp.bfloat16)
    up_rows = jnp.dot(second_norm, up_matrix, preferred_element_type=jnp.float32)
    hidden = gelu_tanh(up_rows).astype(jnp.bfloat16)
    outputs = middle + jnp.dot(hidden, down_matrix, preferred_element_type=jnp.float32)
    kept = (
        inputs,
        normed,
        qkv_rows,
        None,
        attended,
        log_total,
        attended_low,
        middle,
        second_norm,
        up_rows,
        hidden,
        query_segment,
        key_segment,
        keep_rows,
        lengths,
    )
    return (outputs, kept)


def block_backward(kept, grad_out, gains, qkv_matrix, out_matrix, up_matrix, down_matrix):
    (
        inputs,
        normed,
        qkv_rows,
        gathered,
        attended,
        log_total,
        attended_low,
        middle,
        second_norm,
        up_rows,
        hidden,
        query_segment,
        key_segment,
        keep_rows,
        lengths,
    ) = kept
    row_count, width = inputs.shape
    heads = HEADS
    head_size = width // heads
    scale = head_size ** (-0.5)
    grad_down = jnp.einsum("tf,td->fd", hidden, grad_out, preferred_element_type=jnp.float32)
    grad_hidden = jnp.einsum("td,fd->tf", grad_out, down_matrix, preferred_element_type=jnp.float32)
    unused, gelu_back = jax.vjp(gelu_tanh, up_rows)
    grad_up_rows = gelu_back(grad_hidden)[0].astype(jnp.bfloat16)
    grad_up = jnp.einsum("td,tf->df", second_norm, grad_up_rows, preferred_element_type=jnp.float32)
    grad_second = jnp.einsum(
        "tf,df->td", grad_up_rows, up_matrix, preferred_element_type=jnp.float32
    )
    unused, second_back = jax.vjp(layer_norm, middle, gains[1])
    middle_part, gain_second = second_back(grad_second)
    grad_middle = grad_out.astype(jnp.float32) + middle_part
    grad_branch = grad_middle.astype(jnp.bfloat16)
    grad_outw = jnp.einsum(
        "td,te->de", attended_low, grad_branch, preferred_element_type=jnp.float32
    )
    grad_attended = jnp.einsum(
        "te,de->td", grad_branch, out_matrix, preferred_element_type=jnp.float32
    ).astype(jnp.bfloat16) * keep_rows.astype(jnp.bfloat16)
    grad_heads = grad_attended.reshape(row_count, heads, head_size)
    delta = jnp.sum(
        grad_heads.astype(jnp.float32) * attended.reshape(row_count, heads, head_size), axis=-1
    ).T
    query_heads = qkv_rows[:, :width].reshape(row_count, heads, head_size)
    all_keys, all_values = (
        lax.all_gather(qkv_rows[:, width : 2 * width], "seq", axis=0, tiled=True),
        lax.all_gather(qkv_rows[:, 2 * width :], "seq", axis=0, tiled=True),
    )
    key_heads = all_keys.reshape(-1, heads, head_size)
    value_heads = all_values.reshape(-1, heads, head_size)
    grad_query, key_parts = query_side(
        query_heads,
        key_heads,
        value_heads,
        query_segment,
        key_segment,
        grad_heads,
        log_total,
        delta,
        scale,
    )
    grad_keys, grad_values = (
        lax.psum_scatter(
            key_parts[0].reshape(-1, width).astype(jnp.bfloat16),
            "seq",
            scatter_dimension=0,
            tiled=True,
        ).astype(jnp.float32),
        lax.psum_scatter(
            key_parts[1].reshape(-1, width).astype(jnp.bfloat16),
            "seq",
            scatter_dimension=0,
            tiled=True,
        ).astype(jnp.float32),
    )
    grad_qkv_rows = jnp.concatenate(
        [grad_query.reshape(row_count, width), grad_keys, grad_values], axis=1
    ).astype(jnp.bfloat16)
    grad_qkv = jnp.einsum("td,tf->df", normed, grad_qkv_rows, preferred_element_type=jnp.float32)
    grad_first = jnp.einsum(
        "tf,df->td", grad_qkv_rows, qkv_matrix, preferred_element_type=jnp.float32
    )
    unused, first_back = jax.vjp(layer_norm, inputs, gains[0])
    input_part, gain_first = first_back(grad_first)
    grad_inputs = grad_middle + input_part
    return (
        grad_inputs,
        (jnp.stack([gain_first, gain_second]), grad_qkv, grad_outw, grad_up, grad_down),
    )


def local(
    tokens,
    norm_gains,
    qkv_weight,
    out_weight,
    up_weight,
    down_weight,
    gen_cotangent,
    disc_cotangent,
    seg_lengths,
):
    gen_weights = (norm_gains[0], qkv_weight[0], out_weight[0], up_weight[0], down_weight[0])
    disc_weights = (norm_gains[1], qkv_weight[1], out_weight[1], up_weight[1], down_weight[1])
    gen_outs, disc_outs, gen_ins, disc_ins = ([], [], [], [])
    number = 0
    lengths = seg_lengths[number]
    gen_rows, gen_kept = block_forward(tokens[number].astype(jnp.float32), *gen_weights, lengths)
    gen_low = gen_rows.astype(jnp.bfloat16)
    disc_rows, disc_kept = block_forward(gen_low.astype(jnp.float32), *disc_weights, lengths)
    disc_grad_in, disc_terms = block_backward(disc_kept, disc_cotangent[number], *disc_weights)
    gen_grad_in, gen_terms = block_backward(gen_kept, gen_cotangent[number], *gen_weights)
    gen_outs.append(gen_low)
    disc_outs.append(disc_rows.astype(jnp.bfloat16))
    gen_ins.append(gen_grad_in.astype(jnp.bfloat16))
    disc_ins.append(disc_grad_in.astype(jnp.bfloat16))
    stacked = [jnp.stack([gen_terms[number], disc_terms[number]]) for number in range(5)]
    summed = lax.psum(
        (stacked[0], stacked[1], stacked[2], stacked[3], stacked[4]), ("batch", "seq")
    )
    return (
        jnp.stack(gen_outs),
        jnp.stack(disc_outs),
        jnp.stack(gen_ins),
        jnp.stack(disc_ins),
        summed[0],
        summed[1],
        summed[2],
        summed[3],
        summed[4],
    )


def solution(mesh):
    placed = (
        P("batch", "seq", None),
        P(),
        P(),
        P(),
        P(),
        P(),
        P("batch", "seq", None),
        P("batch", "seq", None),
        P("batch", None),
    )
    return jax.shard_map(
        local,
        mesh=mesh,
        in_specs=placed,
        out_specs=(
            P("batch", "seq", None),
            P("batch", "seq", None),
            P("batch", "seq", None),
            P("batch", "seq", None),
            P(),
            P(),
            P(),
            P(),
            P(),
        ),
        check_vma=False,
    )
```

profile of v0, /device:TPU:0, one launch (start us, length us, event | category | flops | bytes accessed | tf_op | source)
XLA Modules:
  0.0 1109.9 jit_solution(12978267367602182645)
XLA Ops:
  20.4 51.9 %all-gather.5.cloned.1.call-done = bf16[2560,512]{1,0:T(8,128)(2,1)} async-done(((bf16[320,512]{1,0:T(8,128)(2,1)}), bf16[2560,512]{1,0:T(8,128)(2,1)}) %all-gather.5.cloned.1.call-update) | async-done | bytes 2621456 | tf_op jit(solution)/shard_map/all_gather | solution.py:149
  72.3 7.4 reshape.439
  79.7 6.9 copy.62
  86.6 41.7 %all-gather.7.cloned.1.call-done = bf16[2560,512]{1,0:T(8,128)(2,1)} async-done(((bf16[320,512]{1,0:T(8,128)(2,1)}), bf16[2560,512]{1,0:T(8,128)(2,1)}) %all-gather.7.cloned.1.call-update) | async-done | bytes 2621456 | tf_op jit(solution)/shard_map/all_gather | solution.py:148
  128.3 7.4 reshape.440
  135.7 5.6 copy.63
  141.3 41.8 %while.78 = (s32[]{:T(128)}, f32[8,320]{1,0:T(8,128)S(1)}, f32[8,320]{1,0:T(8,128)S(1)}, s32[5,512]{1,0:T(8,128)}, bf16[5,512,8,64]{1,3,2,0:T(8,128)(2,1)S(1)}, ...) while((s32[]{:T(128)}, f32[8,320]{1,0:T(8,128)S(1)}, ...), condition=%wide.region_5.6_spmd.clone, body=%wide.region_2.5_spmd.clone.sunk | while | flops 177126720 | bytes 12036768 | solution.py:75
  183.2 30.3 %while.79 = (s32[]{:T(128)}, f32[320,8,64]{0,2,1:T(8,128)}, bf16[5,512,8,64]{1,3,2,0:T(8,128)(2,1)}, s32[5,512]{1,0:T(8,128)}, bf16[5,512,8,64]{1,3,2,0:T(8,128)...) while((s32[]{:T(128)}, f32[320,8,64]{0,2,1:T(8,128)}, ...), condition=%wide.region_7.8_spmd.clone, body=%wide.region_6.7_spmd.clone.sunk | while | flops 341281600 | bytes 3233954 | solution.py:89
  224.9 5.2 fusion.149
  242.0 67.4 %while.82 = (s32[]{:T(128)}, f32[320,8,64]{0,2,1:T(8,128)}, bf16[5,512,8,64]{1,3,2,0:T(8,128)(2,1)}, bf16[5,512,8,64]{1,3,2,0:T(8,128)(2,1)}, bf16[5,512,8,64]{1...) while((s32[]{:T(128)}, f32[320,8,64]{0,2,1:T(8,128)}, ...), condition=%wide.region_24.25_spmd.clone, body=%wide.region_23.24_spmd.clone.sunk | while | flops 852724544 | bytes 96148344 | solution.py:131
  309.4 7.0 copy.97
  316.4 7.9 reshape.433
  326.1 5.2 copy.96
  331.3 7.8 reshape.431
  339.4 7.5 reshape.441
  347.0 6.8 copy.68
  353.8 7.5 reshape.442
  361.3 5.7 copy.69
  366.9 42.1 %while.80 = (s32[]{:T(128)}, f32[8,320]{1,0:T(8,128)S(1)}, f32[8,320]{1,0:T(8,128)S(1)}, s32[5,512]{1,0:T(8,128)}, bf16[5,512,8,64]{1,3,2,0:T(8,128)(2,1)S(1)}, ...) while((s32[]{:T(128)}, f32[8,320]{1,0:T(8,128)S(1)}, ...), condition=%wide.region_15.16_spmd.clone, body=%wide.region_12.15_spmd.clone.sunk | while | flops 177126720 | bytes 12036768 | solution.py:75
  409.0 30.2 %while.81 = (s32[]{:T(128)}, f32[320,8,64]{0,2,1:T(8,128)}, bf16[5,512,8,64]{1,3,2,0:T(8,128)(2,1)}, s32[5,512]{1,0:T(8,128)}, bf16[5,512,8,64]{1,3,2,0:T(8,128)...) while((s32[]{:T(128)}, f32[320,8,64]{0,2,1:T(8,128)}, ...), condition=%wide.region_17.18_spmd.clone, body=%wide.region_16.17_spmd.clone.sunk | while | flops 341281600 | bytes 3233954 | solution.py:89
  428.6 4.5 fusion.381
  459.8 68.4 %while.83 = (s32[]{:T(128)}, f32[320,8,64]{0,2,1:T(8,128)}, bf16[5,512,8,64]{1,3,2,0:T(8,128)(2,1)}, bf16[5,512,8,64]{1,3,2,0:T(8,128)(2,1)}, bf16[5,512,8,64]{1...) while((s32[]{:T(128)}, f32[320,8,64]{0,2,1:T(8,128)}, ...), condition=%wide.region_33.34_spmd.clone, body=%wide.region_32.33_spmd.clone.sunk | while | flops 852724544 | bytes 96230328 | solution.py:131
  528.2 7.0 copy.99
  535.2 7.8 reshape.437
  544.8 5.2 copy.98
  549.9 7.9 reshape.435
  576.3 6.7 pad_maximum_fusion.1
  588.4 23.5 %reduce-scatter.19.cloned.1.call-done = bf16[320,512]{1,0:T(8,128)(2,1)} async-done(((bf16[2560,512]{1,0:T(8,128)(2,1)}), bf16[320,512]{1,0:T(8,128)(2,1)}) %reduce-scatter.19.cloned.1.call-update) | async-done | bytes 327696
  613.1 71.5 %reduce-scatter.17.cloned.1.call-done = bf16[320,512]{1,0:T(8,128)(2,1)} async-done(((bf16[2560,512]{1,0:T(8,128)(2,1)}), bf16[320,512]{1,0:T(8,128)(2,1)}) %reduce-scatter.17.cloned.1.call-update) | async-done | bytes 327696
  698.3 41.4 %psum.35 = f32[2,2,512]{2,1,0:T(2,128)} all-reduce(f32[2,2,512]{2,1,0:T(2,128)S(1)} %pad_maximum_fusion.10), channel_id=1, replica_groups=mesh['batch'=4,'seq'=8] {'batch','seq'}, use_global_device_ids=true, to_apply=%region_42.43 | all-reduce | flops 2048 | bytes 16384 | tf_op jit(solution)/shard_map/psum | solution.py:304
  744.0 341.4 %all-reduce.3.cloned.1.call-done = (f32[2,512,1536]{2,1,0:T(8,128)}, f32[2,512,512]{2,1,0:T(8,128)}, f32[2,512,2048]{2,1,0:T(8,128)}, f32[2,2048,512]{2,1,0:T(8,128)}) async-done(((f32[2,512,1536]{2,1,0:T(8,128)}, f32[2,512,512]{2,1,0:T(8,128)}, f32[2,512,2048]{2,1,0:T(8,128)}, f32[2,2048,512]{2,1,0:T(8,128)}), (f32[2,512,1536]{2,1,0:T(8,128)}, f32[2,512,512]{2,1,0:T(8,128)}, f32[2,512,2048]{2,1,0:T(8,128)}, ...) | async-done | bytes 25165840 | tf_op jit(solution)/shard_map/psum | solution.py:304
  1085.3 6.6 copy.166
  (626 shorter events, 385.8 us)
Async XLA Ops:
  7.2 65.1 %all-gather.5.cloned.1.call-start = ((), (), s32[]{:S(2)}) async-start(), calls=%async_computation.4 | async-start | bytes 2949120 | tf_op jit(solution)/shard_map/all_gather | solution.py:149
  8.6 212.5 %copy-start.83 = (f32[1,1,512]{2,1,0:T(1,128)}, f32[1,1,512]{2,1,0:T(1,128)S(1)}, u32[]{:S(2)}) copy-start(f32[1,1,512]{2,1,0:T(1,128)S(1)} %get-tuple-element.968) | copy-start | bytes 6148
  8.6 223.1 %copy-start.67 = (f32[1,1,512]{2,1,0:T(1,128)}, f32[1,1,512]{2,1,0:T(1,128)S(1)}, u32[]{:S(2)}) copy-start(f32[1,1,512]{2,1,0:T(1,128)S(1)} %get-tuple-element.966) | copy-start | bytes 6148
  14.8 113.5 %all-gather.7.cloned.1.call-start = ((), (), s32[]{:S(2)}) async-start(), calls=%async_computation.5 | async-start | bytes 2949120 | tf_op jit(solution)/shard_map/all_gather | solution.py:148
  15.5 323.9 %all-gather.9.cloned.1.call-start = ((), (), s32[]{:S(2)}) async-start(), calls=%async_computation.6 | async-start | bytes 2949120 | tf_op jit(solution)/shard_map/all_gather | solution.py:149
  183.2 31.5 %copy-start.18 = (bf16[1,320,512]{2,1,0:T(8,128)(2,1)S(1)}, bf16[1,320,512]{2,1,0:T(8,128)(2,1)}, u32[]{:S(2)}) copy-start(bf16[1,320,512]{2,1,0:T(8,128)(2,1)} %param.21) | copy-start | bytes 983044
  216.2 15.5 %copy-start.62 = (f32[320]{0:T(512)}, f32[320]{0:T(512)S(1)}, u32[]{:S(2)}) copy-start(f32[320]{0:T(512)S(1)} %broadcast_multiply_fusion.2) | copy-start | bytes 3844
  216.4 15.3 %copy-start.64 = (f32[320]{0:T(512)}, f32[320]{0:T(512)S(1)}, u32[]{:S(2)}) copy-start(f32[320]{0:T(512)S(1)} %fusion.272) | copy-start | bytes 3844
  220.8 521.1 %copy-start.30 = (bf16[320,512]{1,0:T(8,128)(2,1)}, bf16[320,512]{1,0:T(8,128)(2,1)S(1)}, u32[]{:S(2)}) copy-start(bf16[320,512]{1,0:T(8,128)(2,1)S(1)} %get-tuple-element.977) | copy-start | bytes 983044
  224.0 129.8 %all-gather.11.cloned.1.call-start = ((), (), s32[]{:S(2)}) async-start(), calls=%async_computation.7 | async-start | bytes 2949120 | tf_op jit(solution)/shard_map/all_gather | solution.py:148
  232.1 8.0 copy-start.73
  238.2 344.8 %reduce-scatter.15.cloned.1.call-start = ((), (), s32[]{:S(2)}) async-start(), calls=%async_computation.9 | async-start | bytes 2949120
  324.3 259.9 %reduce-scatter.13.cloned.1.call-start = ((), (), s32[]{:S(2)}) async-start(), calls=%async_computation.8 | async-start | bytes 2949120
  339.1 272.8 %reduce-scatter.19.cloned.1.call-start = ((), (), s32[]{:S(2)}) async-start(), calls=%async_computation.11 | async-start | bytes 2949120
  442.0 7.5 copy-start.13
  543.1 141.6 %reduce-scatter.17.cloned.1.call-start = ((), (), s32[]{:S(2)}) async-start(), calls=%async_computation.10 | async-start | bytes 2949120
  557.9 527.5 %all-reduce.3.cloned.1.call-start = ((), (), s32[]{:S(2)}) async-start(), calls=%async_computation.12 | async-start | bytes 50331648 | tf_op jit(solution)/shard_map/psum | solution.py:304
  566.9 119.0 %copy-start.54 = (bf16[320,8,64]{0,2,1:T(8,128)(2,1)}, bf16[320,8,64]{0,2,1:T(8,128)(2,1)S(1)}, u32[]{:S(2)}) copy-start(bf16[320,8,64]{0,2,1:T(8,128)(2,1)S(1)} %multiply_convert_fusion.2) | copy-start | bytes 983044
  576.3 9.1 copy-start.19
  576.3 9.1 copy-start.53
  576.3 9.2 copy-start.70
  576.3 9.2 copy-start.80
  576.3 9.2 copy-start.86
  585.5 100.4 %copy-start.72 = (f32[320]{0:T(512)S(1)}, f32[320]{0:T(512)}, u32[]{:S(2)}) copy-start(f32[320]{0:T(512)} %copy-done.71) | copy-start | bytes 3844
  585.5 100.4 %copy-start.82 = (f32[320]{0:T(512)S(1)}, f32[320]{0:T(512)}, u32[]{:S(2)}) copy-start(f32[320]{0:T(512)} %copy-done.81) | copy-start | bytes 3844
  585.5 100.4 %copy-start.84 = (f32[1,1,512]{2,1,0:T(1,128)S(1)}, f32[1,1,512]{2,1,0:T(1,128)}, u32[]{:S(2)}) copy-start(f32[1,1,512]{2,1,0:T(1,128)} %copy-done.83) | copy-start | bytes 6148
  613.1 74.0 %copy-start.56 = (bf16[320,512]{0,1:T(8,128)(2,1)}, bf16[320,512]{0,1:T(8,128)(2,1)S(1)}, u32[]{:S(2)}) copy-start(bf16[320,512]{0,1:T(8,128)(2,1)S(1)} %copy.87) | copy-start | bytes 983044
  696.6 43.2 %copy-start.27 = (f32[320,512]{1,0:T(8,128)S(1)}, f32[320,512]{1,0:T(8,128)}, u32[]{:S(2)}) copy-start(f32[320,512]{1,0:T(8,128)} %copy-done.26) | copy-start | bytes 1966084
  696.6 43.2 %copy-start.74 = (f32[320]{0:T(512)S(1)}, f32[320]{0:T(512)}, u32[]{:S(2)}) copy-start(f32[320]{0:T(512)} %copy-done.73) | copy-start | bytes 3844
  697.5 44.4 %copy-start.29 = (f32[320,512]{1,0:T(8,128)S(1)}, f32[320,512]{1,0:T(8,128)}, u32[]{:S(2)}) copy-start(f32[320,512]{1,0:T(8,128)} %copy-done.28) | copy-start | bytes 1966084
  1085.3 6.6 copy-start.34
  1085.3 8.9 copy-start.17
  (131 other events, 352.4 us)
Sparse Core Ops, SparseCore 0:
  14.9 57.3 all-gather.4
  75.0 53.2 all-gather.6
  224.1 53.2 all-gather.8
  280.0 53.2 all-gather.10
  336.7 69.2 reduce-scatter.14
  409.4 69.3 reduce-scatter.12
  543.2 68.6 reduce-scatter.18
  615.4 69.1 reduce-scatter.16
  692.2 393.0 all-reduce.2
where the time goes:
time: 1120 us; the launch traced here: 1110 us
  waiting for transfers between devices  531 us (47%)
  matrix products  236 us (21%)
  local copies, waits for them, and re-layouts  190 us (17%)
  other arithmetic  91.8 us (8%)
  blocking collectives  41.4 us (4%)
  between operations  17.1 us (2%)
    psum x1, waiting for transfers between devices, local(): lax.psum((stacked[0], stacked[1], stacked[2], stacked[3], stacked[4]), ('...  341 us
    unnamed x188, local copies, waits for them, and re-layouts  115 us
    unnamed x13, waiting for transfers between devices  95.9 us
    all_gather x2, waiting for transfers between devices, block_forward(): lax.all_gather(qkv_rows[:, 2 * width:], 'seq', axis=0, tiled=True)  51.9 us
    dot_general x10, matrix products, weighted(): jnp.einsum('hqk,khe->qhe', weights_low, item[1], preferred_element_type=j...  44.6 us
    dot_general x20, matrix products, block_scores(): jnp.einsum('qhe,khe->hqk', query_heads, key_heads, preferred_element_type...  43.2 us
    all_gather x2, waiting for transfers between devices, block_forward(): lax.all_gather(qkv_rows[:, width:2 * width], 'seq', axis=0, tiled=True)  41.7 us
    psum x1, blocking collectives, local(): lax.psum((stacked[0], stacked[1], stacked[2], stacked[3], stacked[4]), ('...  41.4 us
  transfers between devices with their start and end apart: 9, of which 5 were waited for; matrix products, arithmetic and copies ran while one was open for 34% of the time, Pallas kernels for 0%

commit v1 on v0

--- a/solution.py
+++ b/solution.py
@@ -1,8 +1,11 @@
+import functools
 import math
 
 import jax
 import jax.numpy as jnp
 from jax import lax
+from jax.experimental import pallas as pl
+from jax.experimental.pallas import tpu as pltpu
 from jax.sharding import PartitionSpec as P
 
 HEADS = 8
@@ -275,7 +278,7 @@
     )
 
 
-def local(
+def local_scan(
     tokens,
     norm_gains,
     qkv_weight,
@@ -317,6 +320,529 @@
     )
 
 
+NN = (((1,), (0,)), ((), ()))
+NT = (((1,), (1,)), ((), ()))
+TN = (((0,), (0,)), ((), ()))
+LOW = jnp.bfloat16
+WIDE = jnp.float32
+GROUP = 4
+vmem_bytes = 62 << 20
+
+
+def product(left, right, form):
+    return lax.dot_general(left, right, form, preferred_element_type=WIDE)
+
+
+def normalise(inputs):
+    average = jnp.mean(inputs, axis=-1, keepdims=True)
+    centred = inputs - average
+    variance = jnp.mean(centred * centred, axis=-1, keepdims=True)
+    inverse = lax.rsqrt(variance + epsilon)
+    return (centred * inverse, inverse)
+
+
+def normalise_back(hat, inverse, gain_row, grad):
+    scaled = grad * gain_row
+    first = jnp.mean(scaled, axis=-1, keepdims=True)
+    second = jnp.mean(scaled * hat, axis=-1, keepdims=True)
+    return inverse * (scaled - first - hat * second)
+
+
+def segments(lengths, positions):
+    first = lengths[0, 0]
+    second = first + lengths[0, 1]
+    third = second + lengths[0, 2]
+    return (
+        (positions >= first).astype(jnp.int32)
+        + (positions >= second).astype(jnp.int32)
+        + (positions >= third).astype(jnp.int32)
+    )
+
+
+def stacked_positions(band, rows):
+    lanes = lax.broadcasted_iota(jnp.int32, (1, GROUP * rows), 1)
+    for unused in range(1, GROUP):
+        lanes = lanes - jnp.where(lanes >= rows, rows, 0)
+    return lanes + band * rows
+
+
+def head_lanes(rows, head_size):
+    return lax.broadcasted_iota(jnp.int32, (rows, GROUP * head_size), 1) // head_size
+
+
+def stack_heads(rows_group, lane_head):
+    zero = jnp.zeros_like(rows_group)
+    return jnp.concatenate(
+        [jnp.where(lane_head == head, rows_group, zero) for head in range(GROUP)], axis=0
+    )
+
+
+def unstack_heads(stacked, lane_head, rows):
+    total = jnp.where(lane_head == 0, stacked[:rows], 0.0)
+    for head in range(1, GROUP):
+        total = jnp.where(lane_head == head, stacked[head * rows : (head + 1) * rows], total)
+    return total
+
+
+def key_chunks(bands, rows):
+    step = 2 if (bands - 2) % 2 == 0 else 1
+    chunks = [(0, rows)]
+    for at in range(1, bands - 1, step):
+        chunks.append((at * rows, step * rows))
+    chunks.append(((bands - 1) * rows, rows))
+    return chunks
+
+
+def forward_kernel(
+    block,
+    lengths,
+    normed_all,
+    inputs_ref,
+    gains_ref,
+    qkv_hbm,
+    out_hbm,
+    up_hbm,
+    down_hbm,
+    output_ref,
+    next_ref,
+    kv_ref,
+    query_ref,
+    weights_hbm,
+    low_ref,
+    attended_ref,
+    inverse_ref,
+    middle_ref,
+    second_ref,
+    hidden_ref,
+    slope_ref,
+    qkv_matrix,
+    out_matrix,
+    up_matrix,
+    down_matrix,
+    query_stack,
+    scores_ref,
+    weights_ref,
+    load_sems,
+    store_sems,
+):
+    loads = [
+        pltpu.make_async_copy(source.at[block], target, load_sems.at[number])
+        for number, (source, target) in enumerate(
+            [
+                (qkv_hbm, qkv_matrix),
+                (out_hbm, out_matrix),
+                (up_hbm, up_matrix),
+                (down_hbm, down_matrix),
+            ]
+        )
+    ]
+    for load in loads:
+        load.start()
+    rows, width = inputs_ref.shape
+    total = normed_all.shape[0]
+    head_size = width // HEADS
+    group_width = GROUP * head_size
+    groups = width // group_width
+    band = lax.axis_index("seq")
+    lane_head = head_lanes(rows, head_size)
+    chunks = key_chunks(total // rows, rows)
+    image_query = segments(lengths, stacked_positions(band, rows))
+    loads[0].wait()
+    own = normed_all[pl.ds(pl.multiple_of(band * rows, rows), rows), :]
+    query = product(own, qkv_matrix[:, :width], NN).astype(LOW)
+    query = query * jnp.asarray(head_size ** (-0.5), LOW)
+    query_ref[...] = query
+    for group in range(groups):
+        lanes = slice(group * group_width, (group + 1) * group_width)
+        query_stack[group] = stack_heads(query[:, lanes], lane_head)
+    kv_ref[...] = product(normed_all[...], qkv_matrix[:, width:], NN).astype(LOW)
+    stores = []
+    for group in range(groups):
+        lanes = slice(group * group_width, (group + 1) * group_width)
+        value_lanes = slice(width + group * group_width, width + (group + 1) * group_width)
+        stack = query_stack[group]
+        edge_max = None
+        middle_max = None
+        for number, (start, size) in enumerate(chunks):
+            scores = product(kv_ref[start : start + size, lanes], stack, NT)
+            edge = number in (0, len(chunks) - 1)
+            if edge:
+                positions = start + lax.broadcasted_iota(jnp.int32, (size, 1), 0)
+                allowed = segments(lengths, positions) == image_query
+                scores = jnp.where(allowed, scores, masked_score)
+            scores_ref[start : start + size] = scores
+            top = jnp.max(scores, axis=0, keepdims=True)
+            if edge:
+                edge_max = top if edge_max is None else jnp.maximum(edge_max, top)
+            else:
+                middle_max = top if middle_max is None else jnp.maximum(middle_max, top)
+        is_image = image_query == 1
+        row_max = jnp.maximum(edge_max, jnp.where(is_image, middle_max, masked_score))
+        inner_max = jnp.where(is_image, row_max, -masked_score)
+        totals = None
+        gathered = None
+        for number, (start, size) in enumerate(chunks):
+            edge = number in (0, len(chunks) - 1)
+            weights = jnp.exp(scores_ref[start : start + size] - (row_max if edge else inner_max))
+            part = jnp.sum(weights, axis=0, keepdims=True)
+            totals = part if totals is None else totals + part
+            low = weights.astype(LOW)
+            weights_ref[group, start : start + size] = low
+            piece = product(low, kv_ref[start : start + size, value_lanes], TN)
+            gathered = piece if gathered is None else gathered + piece
+        store = pltpu.make_async_copy(
+            weights_ref.at[group], weights_hbm.at[group], store_sems.at[group]
+        )
+        store.start()
+        stores.append(store)
+        columns = jnp.transpose(jnp.broadcast_to(1.0 / totals, (128, GROUP * rows)))
+        inverse = jnp.concatenate([columns] * (group_width // 128), axis=1)
+        attended_ref[:, lanes] = unstack_heads(gathered * inverse, lane_head, rows)
+        inverse_ref[:, lanes] = unstack_heads(inverse, lane_head, rows)
+    positions = band * rows + lax.broadcasted_iota(jnp.int32, (rows, 1), 0)
+    keep_rows = (segments(lengths, positions) < 3).astype(WIDE)
+    low = (attended_ref[...] * keep_rows).astype(LOW)
+    low_ref[...] = low
+    loads[1].wait()
+    middle = inputs_ref[...].astype(WIDE) + product(low, out_matrix[...], NN)
+    middle_ref[...] = middle
+    hat, unused = normalise(middle)
+    second = (hat * gains_ref[block, 1:2, :]).astype(LOW)
+    second_ref[...] = second
+    loads[2].wait()
+    up_rows = product(second, up_matrix[...], NN)
+    square = up_rows * up_rows
+    bend = jnp.tanh(0.7978845608028654 * (up_rows + 0.044715 * square * up_rows))
+    half = 0.5 * (1.0 + bend)
+    hidden = (up_rows * half).astype(LOW)
+    hidden_ref[...] = hidden
+    slope_ref[...] = (
+        half
+        + 0.5
+        * up_rows
+        * (1.0 - bend * bend)
+        * (0.7978845608028654 * (1.0 + (3 * 0.044715) * square))
+    ).astype(LOW)
+    loads[3].wait()
+    output = (middle + product(hidden, down_matrix[...], NN)).astype(LOW)
+    output_ref[...] = output
+    if next_ref is not None:
+        hat, unused = normalise(output.astype(WIDE))
+        next_ref[...] = (hat * gains_ref[block + 1, 0:1, :]).astype(LOW)
+    for store in stores:
+        store.wait()
+
+
+def backward_kernel(
+    block,
+    lengths,
+    normed_all,
+    grad_ref,
+    gains_ref,
+    kv_ref,
+    query_ref,
+    weights_hbm,
+    low_ref,
+    attended_ref,
+    inverse_ref,
+    middle_ref,
+    second_ref,
+    hidden_ref,
+    slope_ref,
+    qkv_hbm,
+    out_hbm,
+    up_hbm,
+    down_hbm,
+    terms_ref,
+    gain_terms_ref,
+    normed_grad_ref,
+    query_grad_ref,
+    middle_grad_ref,
+    qkv_matrix,
+    out_matrix,
+    up_matrix,
+    down_matrix,
+    weights_ref,
+    query_stack,
+    grad_stack,
+    kv_grad_ref,
+    load_sems,
+):
+    loads = [
+        pltpu.make_async_copy(source, target, load_sems.at[number])
+        for number, (source, target) in enumerate(
+            [
+                (down_hbm.at[block], down_matrix),
+                (up_hbm.at[block], up_matrix),
+                (out_hbm.at[block], out_matrix),
+                (weights_hbm, weights_ref),
+                (qkv_hbm.at[block], qkv_matrix),
+            ]
+        )
+    ]
+    for load in loads:
+        load.start()
+    rows, width = grad_ref.shape
+    total = normed_all.shape[0]
+    head_size = width // HEADS
+    group_width = GROUP * head_size
+    groups = width // group_width
+    band = lax.axis_index("seq")
+    lane_head = head_lanes(rows, head_size)
+    chunks = key_chunks(total // rows, rows)
+    fan = hidden_ref.shape[1]
+    qkv_at, out_at, up_at, down_at = 0, 3 * width, 4 * width, 4 * width + fan
+
+    def put(at, value):
+        for number in range(value.shape[1] // width):
+            terms_ref[at + number * width : at + (number + 1) * width] = value[
+                :, number * width : (number + 1) * width
+            ].astype(LOW)
+
+    grad = grad_ref[...]
+    loads[0].wait()
+    grad_hidden = product(grad, down_matrix[...], NT)
+    grad_up = (grad_hidden * slope_ref[...].astype(WIDE)).astype(LOW)
+    terms_ref[down_at : down_at + fan] = product(hidden_ref[...], grad, TN).astype(LOW)
+    put(up_at, product(second_ref[...], grad_up, TN))
+    loads[1].wait()
+    grad_second = product(grad_up, up_matrix[...], NT)
+    hat, inverse = normalise(middle_ref[...])
+    gain_terms_ref[1:2, :] = jnp.sum(grad_second * hat, axis=0, keepdims=True)
+    grad_middle = grad.astype(WIDE) + normalise_back(
+        hat, inverse, gains_ref[block, 1:2, :], grad_second
+    )
+    middle_grad_ref[...] = grad_middle
+    grad_branch = grad_middle.astype(LOW)
+    put(out_at, product(low_ref[...], grad_branch, TN))
+    positions = band * rows + lax.broadcasted_iota(jnp.int32, (rows, 1), 0)
+    keep_rows = (segments(lengths, positions) < 3).astype(WIDE)
+    loads[2].wait()
+    grad_attended = product(grad_branch, out_matrix[...], NT) * keep_rows
+    scaled = (grad_attended * inverse_ref[...]).astype(LOW)
+    ones = jnp.ones((8, group_width), LOW)
+    deltas = []
+    for group in range(groups):
+        lanes = slice(group * group_width, (group + 1) * group_width)
+        query_stack[group] = stack_heads(query_ref[:, lanes], lane_head)
+        stack = stack_heads(scaled[:, lanes], lane_head)
+        grad_stack[group] = stack
+        attended = attended_ref[:, lanes]
+        dots = stack.astype(WIDE) * jnp.concatenate([attended] * GROUP, axis=0)
+        high = dots.astype(LOW)
+        rest = (dots - high.astype(WIDE)).astype(LOW)
+        deltas.append((product(ones, high, NT) + product(ones, rest, NT))[0:1])
+    loads[3].wait()
+    query_grads = []
+    for group in range(groups):
+        lanes = slice(group * group_width, (group + 1) * group_width)
+        value_lanes = slice(width + group * group_width, width + (group + 1) * group_width)
+        collected = None
+        for start, size in chunks:
+            at = slice(start, start + size)
+            low = weights_ref[group, at]
+            grad_weights = product(kv_ref[at, value_lanes], grad_stack[group], NT)
+            grad_scores = (low.astype(WIDE) * (grad_weights - deltas[group])).astype(LOW)
+            kv_grad_ref[at, value_lanes] = product(low, grad_stack[group], NN).astype(LOW)
+            kv_grad_ref[at, lanes] = product(grad_scores, query_stack[group], NN).astype(LOW)
+            piece = product(grad_scores, kv_ref[at, lanes], TN)
+            collected = piece if collected is None else collected + piece
+        query_grads.append(unstack_heads(collected, lane_head, rows))
+    query_grad = (jnp.concatenate(query_grads, axis=1) * head_size ** (-0.5)).astype(LOW)
+    loads[4].wait()
+    own = normed_all[pl.ds(pl.multiple_of(band * rows, rows), rows), :]
+    normed_grad = product(kv_grad_ref[...], qkv_matrix[:, width:], NT)
+    normed_grad_ref[...] = normed_grad.astype(LOW)
+    query_part = product(query_grad, qkv_matrix[:, :width], NT)
+    query_grad_ref[...] = query_part
+    gain_terms_ref[0:1, :] = (
+        jnp.sum(normed_grad * normed_all[...].astype(WIDE), axis=0, keepdims=True)
+        + jnp.sum(query_part * own.astype(WIDE), axis=0, keepdims=True)
+    ) / gains_ref[block, 0:1, :]
+    put(qkv_at, product(own, query_grad, TN))
+    put(qkv_at + width, product(normed_all[...], kv_grad_ref[...], TN))
+
+
+def input_kernel(block, inputs_ref, gains_ref, summed_ref, query_grad_ref, middle_grad_ref, out_ref):
+    hat, inverse = normalise(inputs_ref[...].astype(WIDE))
+    grad = summed_ref[...].astype(WIDE) + query_grad_ref[...]
+    out_ref[...] = (
+        middle_grad_ref[...] + normalise_back(hat, inverse, gains_ref[block, 0:1, :], grad)
+    ).astype(LOW)
+
+
+whole = pl.BlockSpec(memory_space=pltpu.VMEM)
+scalars = pl.BlockSpec(memory_space=pltpu.SMEM)
+apart = pl.BlockSpec(memory_space=pl.ANY)
+
+
+def weight_scratch(width, fan):
+    return {
+        "qkv": pltpu.VMEM((width, 3 * width), LOW),
+        "out": pltpu.VMEM((width, width), LOW),
+        "up": pltpu.VMEM((width, fan), LOW),
+        "down": pltpu.VMEM((fan, width), LOW),
+    }
+
+
+def run_forward(block, lengths, normed_all, inputs, gains, matrices, last):
+    rows, width = inputs.shape
+    total = normed_all.shape[0]
+    fan = matrices[2].shape[2]
+    group_width = GROUP * width // HEADS
+    groups = width // group_width
+    shape = jax.ShapeDtypeStruct
+    outs = [
+        (shape((rows, width), LOW), whole),
+        (shape((rows, width), LOW), whole),
+        (shape((total, 2 * width), LOW), whole),
+        (shape((rows, width), LOW), whole),
+        (shape((groups, total, GROUP * rows), LOW), apart),
+        (shape((rows, width), LOW), whole),
+        (shape((rows, width), WIDE), whole),
+        (shape((rows, width), WIDE), whole),
+        (shape((rows, width), WIDE), whole),
+        (shape((rows, width), LOW), whole),
+        (shape((rows, fan), LOW), whole),
+        (shape((rows, fan), LOW), whole),
+    ]
+    kernel = functools.partial(forward_kernel, block)
+    if last:
+        outs.pop(1)
+
+        def kernel(*refs):
+            forward_kernel(block, *refs[:9], None, *refs[9:])
+
+    held = weight_scratch(width, fan)
+    results = pl.pallas_call(
+        kernel,
+        out_shape=[out[0] for out in outs],
+        in_specs=[scalars, whole, whole, whole, apart, apart, apart, apart],
+        out_specs=[out[1] for out in outs],
+        scratch_shapes=[
+            held["qkv"],
+            held["out"],
+            held["up"],
+            held["down"],
+            pltpu.VMEM((groups, GROUP * rows, group_width), LOW),
+            pltpu.VMEM((total, GROUP * rows), WIDE),
+            pltpu.VMEM((groups, total, GROUP * rows), LOW),
+            pltpu.SemaphoreType.DMA((4,)),
+            pltpu.SemaphoreType.DMA((groups,)),
+        ],
+        compiler_params=pltpu.CompilerParams(vmem_limit_bytes=vmem_bytes),
+        cost_estimate=pl.CostEstimate(flops=14 << 30, bytes_accessed=40 << 20, transcendentals=0),
+        name="forward_part",
+    )(lengths, normed_all, inputs, gains, *matrices)
+    results = list(results)
+    if last:
+        results.insert(1, None)
+    return results
+
+
+def run_backward(block, lengths, normed_all, grad, gains, kept, matrices):
+    rows, width = grad.shape
+    total = normed_all.shape[0]
+    fan = matrices[2].shape[2]
+    group_width = GROUP * width // HEADS
+    groups = width // group_width
+    shape = jax.ShapeDtypeStruct
+    terms = 4 * width + 2 * fan
+    held = weight_scratch(width, fan)
+    return pl.pallas_call(
+        functools.partial(backward_kernel, block),
+        out_shape=[
+            shape((terms, width), LOW),
+            shape((2, width), WIDE),
+            shape((total, width), LOW),
+            shape((rows, width), WIDE),
+            shape((rows, width), WIDE),
+        ],
+        in_specs=[scalars, whole, whole, whole, whole, whole, apart] + [whole] * 7 + [apart] * 4,
+        out_specs=[whole] * 5,
+        scratch_shapes=[
+            held["qkv"],
+            held["out"],
+            held["up"],
+            held["down"],
+            pltpu.VMEM((groups, total, GROUP * rows), LOW),
+            pltpu.VMEM((groups, GROUP * rows, group_width), LOW),
+            pltpu.VMEM((groups, GROUP * rows, group_width), LOW),
+            pltpu.VMEM((total, 2 * width), LOW),
+            pltpu.SemaphoreType.DMA((5,)),
+        ],
+        compiler_params=pltpu.CompilerParams(vmem_limit_bytes=vmem_bytes),
+        cost_estimate=pl.CostEstimate(flops=28 << 30, bytes_accessed=40 << 20, transcendentals=0),
+        name="backward_part",
+    )(lengths, normed_all, grad, gains, *kept, *matrices)
+
+
+def run_input(block, inputs, gains, summed, query_grad, middle_grad):
+    return pl.pallas_call(
+        functools.partial(input_kernel, block),
+        out_shape=jax.ShapeDtypeStruct(inputs.shape, LOW),
+        in_specs=[whole] * 5,
+        out_specs=whole,
+        compiler_params=pltpu.CompilerParams(vmem_limit_bytes=vmem_bytes),
+        name="input_part",
+    )(inputs, gains, summed, query_grad, middle_grad)
+
+
+def local_kernels(
+    tokens,
+    norm_gains,
+    qkv_weight,
+    out_weight,
+    up_weight,
+    down_weight,
+    gen_cotangent,
+    disc_cotangent,
+    seg_lengths,
+):
+    matrices = (qkv_weight, out_weight, up_weight, down_weight)
+    inputs = tokens[0]
+    normed = layer_norm(inputs.astype(WIDE), norm_gains[0, 0]).astype(LOW)
+    terms, gain_terms, outs, ins = ([], [], [], [])
+    for block, grad in enumerate((gen_cotangent[0], disc_cotangent[0])):
+        normed_all = lax.all_gather(normed, "seq", axis=0, tiled=True)
+        output, normed, *kept = run_forward(
+            block, seg_lengths, normed_all, inputs, norm_gains, matrices, block == 1
+        )
+        part, gain_part, normed_grad, query_grad, middle_grad = run_backward(
+            block, seg_lengths, normed_all, grad, norm_gains, kept, matrices
+        )
+        summed = lax.psum_scatter(normed_grad, "seq", scatter_dimension=0, tiled=True)
+        ins.append(run_input(block, inputs, norm_gains, summed, query_grad, middle_grad))
+        outs.append(output)
+        terms.append(lax.psum(part, ("batch", "seq")))
+        gain_terms.append(gain_part)
+        inputs = output
+    width, fan = up_weight.shape[1:]
+
+    def columns(at, count):
+        return jnp.stack(
+            [
+                jnp.concatenate(
+                    [term[at + n * width : at + (n + 1) * width] for n in range(count)], axis=1
+                ).astype(WIDE)
+                for term in terms
+            ]
+        )
+
+    down_at = 4 * width + fan
+    return (
+        outs[0][None],
+        outs[1][None],
+        ins[0][None],
+        ins[1][None],
+        lax.psum(jnp.stack(gain_terms), ("batch", "seq")),
+        columns(0, 3),
+        columns(3 * width, 1),
+        columns(4 * width, fan // width),
+        jnp.stack([term[down_at : down_at + fan] for term in terms]).astype(WIDE),
+    )
+
+
 def solution(mesh):
     placed = (
         P("batch", "seq", None),
@@ -329,8 +855,9 @@
         P("batch", "seq", None),
         P("batch", None),
     )
+    small = mesh.shape["seq"] <= 8
     return jax.shard_map(
-        local,
+        local_kernels if small else local_scan,
         mesh=mesh,
         in_specs=placed,
         out_specs=(

time: 1120 us -> 571 us (0.51)
  matrix products: 236 us -> 0 us
  waiting for transfers between devices: 531 us -> 341 us
  local copies, waits for them, and re-layouts: 190 us -> 7.59 us
  Pallas kernels: 0 us -> 141 us
  other arithmetic: 91.8 us -> 16.6 us
    dot_general x94 -> x0, matrix products: 236 us -> none  [the longest x10 44.6 us: weighted(): jnp.einsum('hqk,khe->qhe', weights_low, item[1], preferred_element_type=j...]
    pallas_call x0 -> x6, Pallas kernels: none -> 141 us  [the longest x2 76 us: run_backward(): pl.pallas_call(functools.partial(backward_kernel, block), out_shape=[shap...]
    unnamed x188 -> x6, local copies, waits for them, and re-layouts: 115 us -> 1.54 us
    psum x1, waiting for transfers between devices: 341 us -> 234 us  [local_kernels(): terms.append(lax.psum(part, ('batch', 'seq')))]
    unnamed x13 -> x5, waiting for transfers between devices: 95.9 us -> 0.58 us
    reduce_sum x15 -> x0, other arithmetic: 37.2 us -> none  [the longest x10 33.2 us: statistics(): jnp.sum(jnp.exp(scores - new_max[..., None]), axis=-1)]
    another operation x8 -> x1, local copies, waits for them, and re-layouts: 37.4 us -> 2.65 us  [local_kernels(): jnp.stack([term[down_at:down_at + fan] for term in terms]).astype(WIDE)]
    reduce_scatter x0 -> x2, waiting for transfers between devices: none -> 34 us  [local_kernels(): lax.psum_scatter(normed_grad, 'seq', scatter_dimension=0, tiled=True)]
  transfers between devices with their start and end apart: 9 -> 5, of which waited for: 5 -> 4; matrix products, arithmetic and copies ran while one was open for 34% -> 0% of each run, Pallas kernels for 0% -> 20%
where the time goes in v1:
time: 571 us; the launch traced here: 562 us
  waiting for transfers between devices  341 us (60%)
  Pallas kernels  141 us (25%)
  blocking collectives  40.4 us (7%)
  other arithmetic  16.6 us (3%)
  between operations  14 us (2%)
  local copies, waits for them, and re-layouts  7.59 us (1%)
    psum x1, waiting for transfers between devices, local_kernels(): terms.append(lax.psum(part, ('batch', 'seq')))  234 us
    pallas_call x2, Pallas kernels, run_backward(): pl.pallas_call(functools.partial(backward_kernel, block), out_shape=[shap...  76 us
    all_gather x2, waiting for transfers between devices, local_kernels(): normed_all = lax.all_gather(normed, 'seq', axis=0, tiled=True)  72.4 us
    pallas_call x2, Pallas kernels, run_forward(): pl.pallas_call(kernel, out_shape=[out[0] for out in outs], in_specs=[scal...  59.8 us
    psum x1, blocking collectives, local_kernels(): lax.psum(jnp.stack(gain_terms), ('batch', 'seq'))  40.4 us
    reduce_scatter x2, waiting for transfers between devices, local_kernels(): lax.psum_scatter(normed_grad, 'seq', scatter_dimension=0, tiled=True)  34 us
  transfers between devices with their start and end apart: 5, of which 4 were waited for; matrix products, arithmetic and copies ran while one was open for 0% of the time, Pallas kernels for 20%

profile of v1, /device:TPU:0, one launch (start us, length us, event | category | flops | bytes accessed | tf_op | source)
XLA Modules:
  0.0 561.7 jit_solution(7503352752206689324)
XLA Ops:
  7.2 0.0 all-gather.3.cloned.1.call-start
  7.2 1.1 convert_reduce_fusion
  8.3 1.2 fusion.2
  9.6 0.7 slice.57
  10.3 1.9 fusion.4
  12.2 0.0 all-gather.5.cloned.1.call-start
  12.2 57.5 %all-gather.3.cloned.1.call-done.normed_all = bf16[2560,512]{1,0:T(8,128)(2,1)} async-done(((bf16[320,512]{1,0:T(8,128)(2,1)}), bf16[2560,512]{1,0:T(8,128)(2,1)}) %all-gather.3.cloned.1.call-update) | async-done | bytes 2621456 | tf_op jit(solution)/shard_map/all_gather | solution.py:807
  69.7 30.1 %forward_part.2 = (bf16[320,512]{1,0:T(8,128)(2,1)}, bf16[320,512]{1,0:T(8,128)(2,1)}, bf16[2560,1024]{1,0:T(8,128)(2,1)}, bf16[320,512]{1,0:T(8,128)(2,1)}, bf1...) custom-call(s32[1,4]{1,0:T(1,128)} %lengths.5, ...), custom_call_target="tpu_custom_call" | custom-call | flops 15032385536 | bytes 41943040 | tf_op jit(solution)/shard_map/forward_part/pallas_call | solution.py:717
  99.8 0.0 all-gather.5.cloned.1.call-update
  99.8 0.4 reduce-scatter.3.cloned.1.call-start
  100.3 37.9 %backward_part.2 = (bf16[6144,512]{1,0:T(8,128)(2,1)}, f32[2,512]{1,0:T(2,128)}, bf16[2560,512]{1,0:T(8,128)(2,1)}, f32[320,512]{1,0:T(8,128)}, f32[320,512]{1,0:T(8,128)}) custom-call(s32[1,4]{1,0:T(1,128)} %lengths.5, bf16[2560,512]{1,0:T(8,128)(2,1)} %all-gather.3.cloned.1.call-done.normed_all, bf16[320,512]{1,0:T(8,128)(2,1)} %bitcast.57, ...), custom_call_target="tpu_custom_call" | custom-call | flops 30064771072 | bytes 41943040 | tf_op jit(solution)/shard_map/backward_part/pallas_call | solution.py:752
  138.2 0.0 reduce-scatter.3.cloned.1.call-update
  138.2 0.0 reduce-scatter.5.cloned.1.call-start
  138.3 14.9 %all-gather.5.cloned.1.call-done.refs_1_.normed_all = bf16[2560,512]{1,0:T(8,128)(2,1)} async-done(((bf16[320,512]{1,0:T(8,128)(2,1)}), bf16[2560,512]{1,0:T(8,128)(2,1)}) %all-gather.5.cloned.1.call-update) | async-done | bytes 2621456 | tf_op jit(solution)/shard_map/all_gather | solution.py:807
  153.2 29.7 %forward_part.3 = (bf16[320,512]{1,0:T(8,128)(2,1)}, bf16[2560,1024]{1,0:T(8,128)(2,1)}, bf16[320,512]{1,0:T(8,128)(2,1)}, bf16[2,2560,1280]{2,1,0:T(8,128)(2,1)...) custom-call(s32[1,4]{1,0:T(1,128)} %lengths.5, ...), custom_call_target="tpu_custom_call" | custom-call | flops 15032385536 | bytes 41943040 | tf_op jit(solution)/shard_map/forward_part/pallas_call | solution.py:717
  182.9 38.1 %backward_part.3 = (bf16[6144,512]{1,0:T(8,128)(2,1)}, f32[2,512]{1,0:T(2,128)}, bf16[2560,512]{1,0:T(8,128)(2,1)}, f32[320,512]{1,0:T(8,128)}, f32[320,512]{1,0:T(8,128)}) custom-call(s32[1,4]{1,0:T(1,128)} %lengths.5, bf16[2560,512]{1,0:T(8,128)(2,1)} %all-gather.5.cloned.1.call-done.refs_1_.normed_all, bf16[320,512]{1,0:T(8,128)(2,1)} %bitcast.58, ...), custom_call_target="tpu_custom_call" | custom-call | flops 30064771072 | bytes 41943040 | tf_op jit(solution)/shard_map/backward_part/pallas_call | solution.py:752
  221.1 0.0 reduce-scatter.5.cloned.1.call-update
  221.1 0.0 all-reduce.3.cloned.1.call-start
  221.2 0.5 all-reduce.3.cloned.1.call-update
  221.7 0.1 copy-done.1
  221.8 40.4 %psum.21 = f32[2,2,512]{2,1,0:T(2,128)} all-reduce(f32[2,2,512]{2,1,0:T(2,128)S(1)} %pad_maximum_fusion), channel_id=1, replica_groups=mesh['batch'=4,'seq'=8] {'batch','seq'}, use_global_device_ids=true, to_apply=%region_4.0 | all-reduce | flops 2048 | bytes 16384 | tf_op jit(solution)/shard_map/psum | solution.py:838
  262.3 2.7 input_part.2
  265.0 34.0 %reduce-scatter.5.cloned.1.call-done.summed_ref = bf16[320,512]{1,0:T(8,128)(2,1)} async-done(((bf16[2560,512]{1,0:T(8,128)(2,1)}), bf16[320,512]{1,0:T(8,128)(2,1)}) %reduce-scatter.5.cloned.1.call-update) | async-done | bytes 327696 | tf_op jit(solution)/shard_map/reduce_scatter | solution.py:814
  299.0 2.7 input_part.3
  301.7 234.2 %all-reduce.3.cloned.1.call-done = (bf16[6144,512]{1,0:T(8,128)(2,1)}, bf16[6144,512]{1,0:T(8,128)(2,1)}) async-done(((bf16[6144,512]{1,0:T(8,128)(2,1)}, bf16[6144,512]{1,0:T(8,128)(2,1)}), (bf16[6144,512]{1,0:T(8,128)(2,1)}, bf16[6144,512]{1,0:T(8,128)(2,1)})) %all-reduce.3.cloned.1.call-update) | async-done | bytes 12582928 | tf_op jit(solution)/shard_map/psum | solution.py:817
  535.9 2.7 slice_bitcast_fusion
  538.6 1.4 copy-done
  540.0 2.7 slice_bitcast_fusion.5
  542.7 1.5 maximum_convert_fusion.3
  544.1 3.9 maximum_convert_fusion.1
  548.1 3.1 maximum_convert_fusion.2
  551.2 3.8 maximum_convert_fusion
  (9 shorter events, 0.0 us)
Async XLA Ops:
  7.2 62.5 %all-gather.3.cloned.1.call-start = ((), (), s32[]{:S(2)}) async-start(), calls=%async_computation.2 | async-start | bytes 2949120 | tf_op jit(solution)/shard_map/all_gather | solution.py:807
  12.2 141.0 %all-gather.5.cloned.1.call-start = ((), (), s32[]{:S(2)}) async-start(), calls=%async_computation.3 | async-start | bytes 2949120 | tf_op jit(solution)/shard_map/all_gather | solution.py:807
  99.8 162.5 %reduce-scatter.3.cloned.1.call-start = ((), (), s32[]{:S(2)}) async-start(), calls=%async_computation.4 | async-start | bytes 2949120 | tf_op jit(solution)/shard_map/reduce_scatter | solution.py:814
  138.2 160.8 %reduce-scatter.5.cloned.1.call-start = ((), (), s32[]{:S(2)}) async-start(), calls=%async_computation.5 | async-start | bytes 2949120 | tf_op jit(solution)/shard_map/reduce_scatter | solution.py:814
  221.1 314.8 %all-reduce.3.cloned.1.call-start = ((), (), s32[]{:S(2)}) async-start(), calls=%async_computation.6 | async-start | bytes 25165824 | tf_op jit(solution)/shard_map/psum | solution.py:817
  221.1 0.7 copy-start.1
  221.1 0.7 copy-start.2
  535.9 4.0 copy-start
Sparse Core Ops, SparseCore 0:
  12.3 57.3 all-gather.2
  99.9 53.2 all-gather.4
  156.7 69.0 reduce-scatter.2
  229.2 69.7 reduce-scatter.4
  306.4 229.4 all-reduce.2
